TPU v7x, 32 devices: a whole 2x2x4 slice. The times are simulated.
32 devices in a mesh: ctx: 8 (over y, x, core), tp: 4 (over z).
Axes of the slice: x: 2, y: 2, z: 4, core: 2. Of those that a mesh axis runs over, the one named last changes fastest.
Arguments:
- hidden: bfloat16 [2048, 8192], P('ctx', 'tp'), may hold values from -6 to 6
- w_feature: bfloat16 [8192, 3, 8192], P('ctx', None, 'tp'), may hold values from -0.0625 to 0.0625
- short_filter: float32 [7, 3, 8192], P(None, None, 'tp'), may hold values from -2.4 to 2.4
- mr_filter: bfloat16 [512, 128], P('tp'), may hold values from -0.5 to 0.5
- w_out: bfloat16 [8192, 8192], P('tp'), may hold values from -0.09375 to 0.09375
Outputs:
- mixed: bfloat16 [2048, 8192], P('ctx', 'tp')
All inputs are finite; a program needn't handle non-finite values.
Results may differ from a plain program's by a relative error of at most 0.024.
Values may be sent and summed in bfloat16 or wider, within the bound.
A program may use at most 128 MiB of HBM per device.

v0:
```python
import jax
import jax.numpy as jnp
from jax import lax
from jax.sharding import PartitionSpec as P

TAPS_SHORT = 7
TAPS_MR = 128
GROUP = 16


def passed_along(value, axis, by):
    count = lax.axis_size(axis)
    pairs = [(i, i + by) for i in range(count) if 0 <= i + by < count]
    return lax.ppermute(value, axis, pairs)


def short_filtering(extended, tap_weights):
    row_count = extended.shape[0] - (TAPS_SHORT - 1)
    running = jnp.zeros((row_count,) + extended.shape[1:], jnp.float32)
    for shift_by in range(TAPS_SHORT):
        row_start = TAPS_SHORT - 1 - shift_by
        running = running + tap_weights[shift_by] * extended[row_start : row_start + row_count]
    return running


def long_filtering(gated_ext, filters, out_count):
    channel_count = gated_ext.shape[1]
    groups = filters.shape[0]
    blocks = -(-out_count // TAPS_MR)
    pad_rows = (blocks + 1) * TAPS_MR - gated_ext.shape[0]
    padded = jnp.pad(gated_ext, ((0, pad_rows), (0, 0)))
    tile_rows = padded.reshape(blocks + 1, TAPS_MR, groups, GROUP)
    windows = jnp.concatenate([tile_rows[:-1], tile_rows[1:]], axis=1)
    out_pos = lax.broadcasted_iota(jnp.int32, (TAPS_MR, 2 * TAPS_MR, TAPS_MR), 0)
    in_pos = lax.broadcasted_iota(jnp.int32, (TAPS_MR, 2 * TAPS_MR, TAPS_MR), 1)
    tap_pos = lax.broadcasted_iota(jnp.int32, (TAPS_MR, 2 * TAPS_MR, TAPS_MR), 2)
    picker = (out_pos + (TAPS_MR - 1) - in_pos == tap_pos).astype(jnp.bfloat16)
    toeplitz = jnp.einsum(
        "asj,gj->gas", picker, filters, preferred_element_type=jnp.float32
    ).astype(jnp.bfloat16)
    result = jnp.einsum("gas,bsgc->bagc", toeplitz, windows, preferred_element_type=jnp.float32)
    return result.reshape(blocks * TAPS_MR, channel_count)


def local(hidden, w_feature, short_filter, mr_filter, w_out):
    block_rows = hidden.shape[0]
    feature_block = w_feature.shape[0]
    slab_width = w_feature.shape[2]
    flat_weight = w_feature.reshape(feature_block, 3 * slab_width)
    gathered = lax.all_gather(hidden, "tp", axis=1, tiled=True)
    feature_cols = lax.all_to_all(gathered, "ctx", split_axis=1, concat_axis=0, tiled=True)
    projected = lax.psum_scatter(
        jnp.dot(feature_cols, flat_weight, preferred_element_type=jnp.float32).astype(jnp.bfloat16),
        "ctx",
        scatter_dimension=0,
        tiled=True,
    ).astype(jnp.float32)
    projected = projected.reshape(block_rows, 3, slab_width)
    rim_rows = passed_along(
        projected[block_rows - (TAPS_SHORT - 1) :].astype(jnp.bfloat16), "ctx", 1
    ).astype(jnp.float32)
    streams = short_filtering(jnp.concatenate([rim_rows, projected], 0), short_filter)
    gated_rows = (streams[:, 1] * streams[:, 2]).astype(jnp.bfloat16)
    gated_rim = passed_along(gated_rows[block_rows - (TAPS_MR - 1) :], "ctx", 1)
    gated_ext = jnp.concatenate([gated_rim, gated_rows], 0)
    queries = streams[:, 0]
    long_out = long_filtering(gated_ext, mr_filter, block_rows)
    mixer_rows = (queries * long_out).astype(jnp.bfloat16)
    summed = lax.psum_scatter(
        lax.dot_general(
            w_out, mixer_rows, (((0,), (1,)), ((), ())), preferred_element_type=jnp.float32
        ).astype(jnp.bfloat16),
        "tp",
        scatter_dimension=0,
        tiled=True,
    ).astype(jnp.float32)
    return summed.T.astype(jnp.bfloat16)


def solution(mesh):
    return jax.shard_map(
        local,
        mesh=mesh,
        in_specs=(
            P("ctx", "tp"),
            P("ctx", None, "tp"),
            P(None, None, "tp"),
            P("tp", None),
            P("tp", None),
        ),
        out_specs=P("ctx", "tp"),
        check_vma=False,
    )
```

profile of v0, /device:TPU:0, one launch (start us, length us, event | category | flops | bytes accessed | tf_op | source)
XLA Modules:
  0.0 518.8 jit_solution(17096268108447489947)
XLA Ops:
  6.5 0.0 copy-start
  6.5 0.0 all-gather.2.cloned.1.call-start
  6.5 2.3 copy.30
  8.8 0.0 all-gather.2.cloned.1.call-update
  8.8 83.6 %all-gather.2.cloned.1.call-done = bf16[256,8192]{0,1:T(8,128)(2,1)} async-done(((bf16[256,2048]{0,1:T(8,128)(2,1)}), bf16[256,8192]{0,1:T(8,128)(2,1)}) %all-gather.2.cloned.1.call-update) | async-done | bytes 4194320 | tf_op jit(solution)/shard_map/all_gather | solution.py:50
  92.4 4.5 all-to-all-start
  97.0 0.0 reduce-scatter.3.cloned.1.call-start
  97.1 16.7 %copy.32 = bf16[1024,3,2048]{0,2,1:T(8,128)(2,1)} copy(bf16[1024,3,2048]{2,0,1:T(8,128)(2,1)} %param.6) | data formatting | bytes 25165824 | tf_op args[1]
  113.7 32.4 %all-to-all-done = bf16[256,8,1024]{0,2,1:T(8,128)(2,1)} async-done(((bf16[256,8,1024]{0,2,1:T(8,128)(2,1)}), bf16[256,8,1024]{0,2,1:T(8,128)(2,1)}, u32[]{:S(2)}, u32[]{:S(2)}) %all-to-all-start) | async-done | bytes 4194336 | tf_op jit(solution)/shard_map/all_to_all | solution.py:51
  146.1 6.5 %copy.31 = bf16[8,256,1024]{2,1,0:T(8,128)(2,1)} copy(bf16[8,256,1024]{1,2,0:T(8,128)(2,1)} %bitcast.1) | data formatting | bytes 8388608 | tf_op jit(solution)/shard_map/all_to_all | solution.py:51
  152.6 33.7 %convolution_convert_fusion = bf16[2048,6144]{1,0:T(8,128)(2,1)} fusion(bf16[2048,1024]{1,0:T(8,128)(2,1)} %bitcast.64, bf16[1024,6144]{0,1:T(8,128)(2,1)} %bitcast.59), kind=kOutput, calls=%fused_computation | convolution fusion | flops 25782386688 | bytes 41943040 | tf_op jit(solution)/shard_map/dot_general | solution.py:53
  186.3 0.0 copy-start.2
  186.3 0.0 reduce-scatter.3.cloned.1.call-update
  186.3 0.0 reduce-scatter.5.cloned.1.call-start
  186.4 0.9 copy-done.2
  187.2 0.1 fusion.33
  187.4 152.7 %reduce-scatter.3.cloned.1.call-done = bf16[256,6144]{1,0:T(8,128)(2,1)} async-done(((bf16[2048,6144]{1,0:T(8,128)(2,1)}), bf16[256,6144]{1,0:T(8,128)(2,1)}) %reduce-scatter.3.cloned.1.call-update) | async-done | bytes 3145744 | tf_op jit(solution)/shard_map/reduce_scatter | solution.py:52
  340.1 0.9 slice.95
  341.1 1.9 collective-permute-start
  343.0 5.4 %copy.33 = f32[256,6144]{0,1:T(8,128)} copy(bf16[256,6144]{1,0:T(8,128)(2,1)} %reduce-scatter.3.cloned.1.call-done) | data formatting | bytes 9437184 | tf_op jit(solution)/shard_map/reshape | solution.py:58
  348.5 0.0 collective-permute-done
  348.5 0.7 copy.35
  349.2 26.3 %fusion.6 = f32[256,3,2048]{0,2,1:T(8,128)S(1)} fusion(f32[256,3,2048]{0,2,1:T(8,128)} %bitcast.58, f32[6,3,2048]{0,2,1:T(8,128)S(1)} %copy.35, f32[3,2048]{1,0:T(4,128)S(1)} %get-tuple-element.12, f32[3,2048]{1,0:T(4,128)S(1)} %get-tuple-element.13, f32[3,2048]{1,0:T(4,128)S(1)} %get-tuple-element.14, f32[3,2048]{1,0:T(4,128)S(1)} %get-tuple-element.15, ...), kind=kLoop, calls=%fused_computation.20 | loop fusion | flops 29884416 | bytes 12902400 | tf_op jit(solution)/shard_map/add | solution.py:22
  375.5 0.0 copy-start.1
  375.5 2.6 copy-done.1
  378.2 0.2 fusion.21
  378.4 0.2 slice_bitcast_fusion.1
  378.6 3.5 collective-permute-start.1
  382.2 0.0 copy-done
  382.2 6.3 %convert_bitcast_fusion = bf16[128,128,256,1]{0,2,1,3:T(8,128)(2,1)} fusion(s32[128]{0:T(128)S(1)} %iota_add_fusion, bf16[128,128]{1,0:T(8,128)(2,1)S(1)} %copy-done), kind=kOutput, calls=%fused_computation.15 | convolution fusion | flops 1086324736 | bytes 8421888 | tf_op jit(solution)/shard_map/asj,gj->gas/dot_general | solution.py:38
  388.4 12.8 %copy.44 = bf16[128,128,256,1]{2,1,3,0:T(8,128)(2,1)} copy(bf16[128,128,256,1]{0,2,1,3:T(8,128)(2,1)} %convert_bitcast_fusion) | data formatting | bytes 16777216 | tf_op jit(solution)/shard_map/convert_element_type | solution.py:40
  401.2 0.6 copy.36
  401.9 0.0 collective-permute-done.1
  401.9 0.3 copy.37
  402.2 1.1 fusion.29
  403.3 0.3 pad_maximum_fusion.1
  403.6 1.5 copy.38
  405.1 1.1 slice.92
  406.2 1.4 copy.40
  407.6 1.0 pad_slice_fusion.12
  408.6 1.5 copy.39
  410.1 0.3 slice.94
  410.4 0.2 copy.41
  410.6 6.3 %fusion.26 = f32[2,128,128,16]{1,3,0,2:T(8,128)S(1)} fusion(bf16[128,128,256,1]{2,1,3,0:T(8,128)(2,1)} %copy.44, bf16[2,128,128,16]{1,3,0,2:T(8,128)(2,1)S(1)} %copy.41, bf16[2,128,128,16]{1,3,0,2:T(8,128)(2,1)S(1)} %copy.40), kind=kOutput, calls=%fused_computation.47 | convolution fusion | flops 272629760 | bytes 12582912 | tf_op jit(solution)/shard_map/gas,bsgc->bagc/dot_general | solution.py:41
  416.9 1.1 copy.43
  418.0 17.3 %fusion.1 = bf16[8192,256]{0,1:T(8,128)(2,1)} fusion(bf16[2048,8192]{1,0:T(8,128)(2,1)} %param.9, f32[256,8,2,128]{3,2,1,0:T(2,128)S(1)} %bitcast.60, f32[256,3,2048]{0,2,1:T(8,128)} %copy-done.1), kind=kOutput, calls=%fused_computation.14 | convolution fusion | flops 8593080320 | bytes 41943040 | tf_op jit(solution)/shard_map/dot_general | solution.py:70
  435.3 0.0 reduce-scatter.5.cloned.1.call-update
  435.3 76.9 %reduce-scatter.5.cloned.1.call-done = bf16[2048,256]{0,1:T(8,128)(2,1)} async-done(((bf16[8192,256]{0,1:T(8,128)(2,1)}), bf16[2048,256]{0,1:T(8,128)(2,1)}) %reduce-scatter.5.cloned.1.call-update) | async-done | bytes 1048592 | tf_op jit(solution)/shard_map/reduce_scatter | solution.py:69
  (5 shorter events, 0.1 us)
Async XLA Ops:
  6.5 375.6 %copy-start = (bf16[128,128]{1,0:T(8,128)(2,1)S(1)}, bf16[128,128]{1,0:T(8,128)(2,1)}, u32[]{:S(2)}) copy-start(bf16[128,128]{1,0:T(8,128)(2,1)} %param.8) | copy-start | bytes 98308
  6.5 85.9 %all-gather.2.cloned.1.call-start = ((), (), s32[]{:S(2)}) async-start(), calls=%async_computation.3 | async-start | bytes 5242880 | tf_op jit(solution)/shard_map/all_gather | solution.py:50
  92.4 53.7 %all-to-all-start = ((bf16[256,8,1024]{0,2,1:T(8,128)(2,1)}), bf16[256,8,1024]{0,2,1:T(8,128)(2,1)}, u32[]{:S(2)}, u32[]{:S(2)}) async-start(bf16[256,8,1024]{0,2,1:T(8,128)(2,1)} %bitcast.63), calls=%async_computation | async-start | bytes 8388608 | tf_op jit(solution)/shard_map/all_to_all | solution.py:51
  97.0 243.1 %reduce-scatter.3.cloned.1.call-start = ((), (), s32[]{:S(2)}) async-start(), calls=%async_computation.4 | async-start | bytes 28311552 | tf_op jit(solution)/shard_map/reduce_scatter | solution.py:52
  186.3 0.9 copy-start.2
  186.3 325.9 %reduce-scatter.5.cloned.1.call-start = ((), (), s32[]{:S(2)}) async-start(), calls=%async_computation.5 | async-start | bytes 5242880 | tf_op jit(solution)/shard_map/reduce_scatter | solution.py:69
  341.1 7.4 %collective-permute-start = (bf16[6,3,2048]{2,0,1:T(8,128)(2,1)S(1)}, bf16[6,3,2048]{2,0,1:T(8,128)(2,1)S(1)}, u32[]{:S(2)}, u32[]{:S(2)}) collective-permute-start(bf16[6,3,2048]{2,0,1:T(8,128)(2,1)S(1)} %bitcast.66), channel_id=1, source_target_pairs={{0,4},{4,8},{8,12},{12,16},{16,20},{20,24},{24,28},{1,5},{5,9},{9,... | collective-permute-start | bytes 221192 | tf_op jit(solution)/shard_map/ppermute | solution.py:14
  375.5 2.6 copy-start.1
  378.6 23.3 %collective-permute-start.1 = (bf16[127,2048]{0,1:T(8,128)(2,1)S(1)}, bf16[127,2048]{0,1:T(8,128)(2,1)S(1)}, u32[]{:S(2)}, u32[]{:S(2)}) collective-permute-start(bf16[127,2048]{0,1:T(8,128)(2,1)S(1)} %slice_bitcast_fusion.1), channel_id=1, source_target_pairs={{0,4},{4,8},{8,12},{12,16},{16,20},{20,24},{24,28},{1,5},{5,9},{9,... | collective-permute-start | bytes 1560584 | tf_op jit(solution)/shard_map/ppermute | solution.py:14
Sparse Core Ops, SparseCore 0:
  9.0 83.4 all-gather.1
  186.5 153.6 reduce-scatter.2
  435.5 76.7 reduce-scatter.4
where the time goes:
time: 520 us; the launch traced here: 519 us
  waiting for transfers between devices  346 us (67%)
  matrix products  63.6 us (12%)
  local copies, waits for them, and re-layouts  58.2 us (11%)
  other arithmetic  28 us (5%)
  between operations  13.3 us (3%)
  starting transfers between devices  10.1 us (2%)
    reduce_scatter x1, waiting for transfers between devices, local(): lax.psum_scatter(jnp.dot(feature_cols, flat_weight, preferred_element_typ...  153 us
    all_gather x1, waiting for transfers between devices, local(): gathered = lax.all_gather(hidden, 'tp', axis=1, tiled=True)  83.6 us
    reduce_scatter x1, waiting for transfers between devices, local(): lax.psum_scatter(lax.dot_general(w_out, mixer_rows, (((0,), (1,)), ((), (...  76.9 us
    dot_general x1, matrix products, local(): jnp.dot(feature_cols, flat_weight, preferred_element_type=jnp.float32)  33.7 us
    all_to_all x1, waiting for transfers between devices, local(): lax.all_to_all(gathered, 'ctx', split_axis=1, concat_axis=0, tiled=True)  32.4 us
    add x1, other arithmetic, short_filtering(): running + tap_weights[shift_by] * extended[row_start:row_start + row_count]  26.3 us
    unnamed x12, local copies, waits for them, and re-layouts  22.5 us
    dot_general x1, matrix products, local(): lax.dot_general(w_out, mixer_rows, (((0,), (1,)), ((), ())), preferred_el...  17.3 us
  transfers between devices with their start and end apart: 6, of which 4 were waited for; matrix products, arithmetic and copies ran while one was open for 8% of the time, Pallas kernels for 0%

commit v1 on v0

v1 whole, which is shorter than its diff:
```python
import functools

import jax
import jax.numpy as jnp
from jax import lax
from jax.experimental import pallas as pl
from jax.experimental.pallas import tpu as pltpu
from jax.sharding import PartitionSpec as P

TAPS_SHORT = 7
TAPS_MR = 128
GROUP = 16
LANES = 128
RIM = 16
VMEM_LIMIT = 48 * 1024 * 1024


def params():
    return pltpu.CompilerParams(vmem_limit_bytes=VMEM_LIMIT)


def passed_along(value, axis, by):
    count = lax.axis_size(axis)
    pairs = [(i, i + by) for i in range(count) if 0 <= i + by < count]
    return lax.ppermute(value, axis, pairs)


def toeplitz_kernel(row_ref, out_ref):
    for g in range(row_ref.shape[0]):
        row = jnp.broadcast_to(row_ref[g : g + 1, :], out_ref.shape[1:])
        out_ref[g] = pltpu.roll(row, 0, 1, stride=1, stride_axis=0).astype(out_ref.dtype)


def toeplitz_of(filters):
    groups = filters.shape[0]
    per = LANES // GROUP
    rows = jnp.pad(filters[:, ::-1].astype(jnp.float32), ((0, 0), (1, TAPS_MR - 1)))
    return pl.pallas_call(
        toeplitz_kernel,
        grid=(groups // per,),
        in_specs=[pl.BlockSpec((per, 2 * TAPS_MR), lambda i: (i, 0))],
        out_specs=pl.BlockSpec((per, TAPS_MR, 2 * TAPS_MR), lambda i: (i, 0, 0)),
        out_shape=jax.ShapeDtypeStruct((groups, TAPS_MR, 2 * TAPS_MR), jnp.bfloat16),
        compiler_params=params(),
        name="toeplitz",
    )(rows)


def short_filtering(rim, value, taps):
    rows = value.shape[0]
    ext = jnp.concatenate([rim.astype(jnp.float32), value.astype(jnp.float32)], 0)
    running = jnp.zeros(value.shape, jnp.float32)
    for shift_by in range(TAPS_SHORT):
        start = rim.shape[0] - shift_by
        running = running + taps[shift_by : shift_by + 1] * ext[start : start + rows]
    return running


def gate_kernel(k_ref, v_ref, kr_ref, vr_ref, kt_ref, vt_ref, out_ref):
    k = short_filtering(kr_ref[...], k_ref[...], kt_ref[...])
    v = short_filtering(vr_ref[...], v_ref[...], vt_ref[...])
    out_ref[...] = (k * v).astype(out_ref.dtype)


def gating(k, v, k_rim, v_rim, k_taps, v_taps):
    rows, width = k.shape
    tile = min(width, 256)
    whole = pl.BlockSpec((rows, tile), lambda i: (0, i))
    rim = pl.BlockSpec((k_rim.shape[0], tile), lambda i: (0, i))
    taps = pl.BlockSpec((TAPS_SHORT, tile), lambda i: (0, i))
    return pl.pallas_call(
        gate_kernel,
        grid=(width // tile,),
        in_specs=[whole, whole, rim, rim, taps, taps],
        out_specs=whole,
        out_shape=jax.ShapeDtypeStruct(k.shape, jnp.bfloat16),
        compiler_params=params(),
        name="gate",
    )(k, v, k_rim, v_rim, k_taps, v_taps)


def long_kernel(g_ref, r_ref, t_ref, out_ref):
    per = t_ref.shape[0]
    ext = jnp.concatenate([r_ref[...], g_ref[...]], 0)
    blocks = g_ref.shape[0] // TAPS_MR
    windows = jnp.concatenate(
        [ext[b * TAPS_MR : (b + 2) * TAPS_MR] for b in range(blocks)], 1
    )
    matrix = t_ref[...].reshape(per * TAPS_MR, 2 * TAPS_MR)
    result = jnp.dot(matrix, windows, preferred_element_type=jnp.float32)
    lane = lax.broadcasted_iota(jnp.int32, (TAPS_MR, blocks * LANES), 1) % LANES // GROUP
    chosen = result[:TAPS_MR]
    for g in range(1, per):
        chosen = jnp.where(lane == g, result[g * TAPS_MR : (g + 1) * TAPS_MR], chosen)
    for b in range(blocks):
        out_ref[b * TAPS_MR : (b + 1) * TAPS_MR] = chosen[:, b * LANES : (b + 1) * LANES]


def long_filtering(gated, rim, toeplitz):
    rows, width = gated.shape
    per = LANES // GROUP
    spec = pl.BlockSpec((rows, LANES), lambda i: (0, i))
    return pl.pallas_call(
        long_kernel,
        grid=(width // LANES,),
        in_specs=[
            spec,
            pl.BlockSpec((TAPS_MR, LANES), lambda i: (0, i)),
            pl.BlockSpec((per, TAPS_MR, 2 * TAPS_MR), lambda i: (i, 0, 0)),
        ],
        out_specs=spec,
        out_shape=jax.ShapeDtypeStruct(gated.shape, jnp.float32),
        compiler_params=params(),
        cost_estimate=pl.CostEstimate(
            flops=4 * rows * width * per * TAPS_MR,
            bytes_accessed=toeplitz.size * 2 + rows * width * 8,
            transcendentals=0,
        ),
        name="long",
    )(gated, rim, toeplitz)


def out_kernel(q_ref, qr_ref, qt_ref, l_ref, w_ref, out_ref, mixer_ref):
    @pl.when(pl.program_id(0) == 0)
    def _():
        width = q_ref.shape[1]
        tile = min(width, 256)
        for at in range(0, width, tile):
            cols = slice(at, at + tile)
            q = short_filtering(qr_ref[:, cols], q_ref[:, cols], qt_ref[:, cols])
            mixer_ref[:, cols] = (q * l_ref[:, cols]).astype(mixer_ref.dtype)

    out_ref[0] = jnp.dot(
        mixer_ref[...], w_ref[...], preferred_element_type=jnp.float32
    ).astype(out_ref.dtype)


def out_projection(q, q_rim, q_taps, long_out, w_out, slabs):
    rows, width = q.shape
    slab = w_out.shape[1] // slabs
    tile = min(slab, 512)
    per = slab // tile
    whole = lambda a: pl.BlockSpec(a.shape, lambda i: (0, 0))
    return pl.pallas_call(
        out_kernel,
        grid=(slabs * per,),
        in_specs=[
            whole(q), whole(q_rim), whole(q_taps), whole(long_out),
            pl.BlockSpec((width, tile), lambda i: (0, i)),
        ],
        out_specs=pl.BlockSpec((1, rows, tile), lambda i: (i // per, 0, i % per)),
        out_shape=jax.ShapeDtypeStruct((slabs, rows, slab), jnp.bfloat16),
        scratch_shapes=[pltpu.VMEM((rows, width), jnp.bfloat16)],
        compiler_params=params(),
        name="out",
    )(q, q_rim, q_taps, long_out, w_out)


def local(hidden, w_feature, short_filter, mr_filter, w_out):
    rows = hidden.shape[0]
    feature_block = w_feature.shape[0]
    n_tp = lax.axis_size("tp")
    n_ctx = lax.axis_size("ctx")
    parts = hidden.shape[1] // feature_block
    blocked = jnp.swapaxes(hidden.reshape(rows, parts, feature_block), 0, 1)
    gathered = lax.all_gather(blocked, "tp", axis=0, tiled=True)
    toeplitz = toeplitz_of(mr_filter)
    gathered, toeplitz = lax.optimization_barrier((gathered, toeplitz))
    columns = lax.all_to_all(gathered, "ctx", split_axis=0, concat_axis=0, tiled=True)
    columns = columns.reshape(n_ctx * rows, feature_block)

    def stream(p, operand):
        partial_sum = jnp.dot(
            operand, w_feature[:, p], preferred_element_type=jnp.float32
        ).astype(jnp.bfloat16)
        return partial_sum

    def scattered(partial_sum):
        return lax.psum_scatter(partial_sum, "ctx", scatter_dimension=0, tiled=True)

    k = scattered(stream(1, columns))
    v = scattered(stream(2, columns))
    q = scattered(stream(0, columns))
    k_rim = passed_along(k[rows - RIM :], "ctx", 1)
    v_rim = passed_along(v[rows - RIM :], "ctx", 1)
    gated = gating(k, v, k_rim, v_rim, short_filter[:, 1], short_filter[:, 2])
    gated_rim = passed_along(gated[rows - TAPS_MR :], "ctx", 1)
    long_out = long_filtering(gated, gated_rim, toeplitz)
    q_rim = passed_along(q[rows - RIM :], "ctx", 1)
    partial_out = out_projection(q, q_rim, short_filter[:, 0], long_out, w_out, n_tp)
    summed = lax.psum_scatter(partial_out, "tp", scatter_dimension=0, tiled=True)
    return summed.reshape(rows, -1)


def solution(mesh):
    return jax.shard_map(
        local,
        mesh=mesh,
        in_specs=(
            P("ctx", "tp"),
            P("ctx", None, "tp"),
            P(None, None, "tp"),
            P("tp", None),
            P("tp", None),
        ),
        out_specs=P("ctx", "tp"),
        check_vma=False,
    )
```

time: 520 us -> 503 us (0.967)
  blocking collectives: 0 us -> 52.8 us
  Pallas kernels: 0 us -> 48.7 us
  local copies, waits for them, and re-layouts: 58.2 us -> 10 us
  other arithmetic: 28 us -> 0.09 us
  matrix products: 63.6 us -> 41.6 us
  waiting for transfers between devices: 346 us -> 326 us
    all_to_all x0 -> x1, blocking collectives: none -> 52.8 us  [local(): lax.all_to_all(gathered, 'ctx', split_axis=0, concat_axis=0, tiled=True)]
    pallas_call x0 -> x4, Pallas kernels: none -> 48.7 us  [the longest x1 23.7 us: out_projection(): pl.pallas_call(out_kernel, grid=(slabs * per,), in_specs=[whole(q), whole...]
    all_to_all x1 -> x0, waiting for transfers between devices: 32.4 us -> none  [local(): lax.all_to_all(gathered, 'ctx', split_axis=1, concat_axis=0, tiled=True)]
    add x2 -> x0, other arithmetic: 26.3 us -> none  [the longest x1 26.3 us: short_filtering(): running + tap_weights[shift_by] * extended[row_start:row_start + row_count]]
    dot_general x4 -> x3, matrix products: 63.6 us -> 41.6 us  [stream(): jnp.dot(operand, w_feature[:, p], preferred_element_type=jnp.float32)]
    reduce_scatter x2 -> x4, waiting for transfers between devices: 230 us -> 250 us  [the longest x3 172 us: scattered(): return lax.psum_scatter(partial_sum, 'ctx', scatter_dimension=0, tiled=True)]
    unnamed x12 -> x13, local copies, waits for them, and re-layouts: 22.5 us -> 6.01 us
    convert_element_type x3 -> x0, local copies, waits for them, and re-layouts: 14.1 us -> none  [the longest x1 12.8 us: long_filtering(): toeplitz = jnp.einsum('asj,gj->gas', picker, filters, preferred_element_t...]
  transfers between devices with their start and end apart: 6 -> 9, of which waited for: 4 -> 6; matrix products, arithmetic and copies ran while one was open for 8% -> 6% of each run, Pallas kernels for 0% -> 5%
where the time goes in v1:
time: 503 us; the launch traced here: 502 us
  waiting for transfers between devices  326 us (65%)
  blocking collectives  52.8 us (10%)
  Pallas kernels  48.7 us (10%)
  matrix products  41.6 us (8%)
  between operations  13.3 us (3%)
  local copies, waits for them, and re-layouts  10 us (2%)
  starting transfers between devices  9.65 us (2%)
    reduce_scatter x3, waiting for transfers between devices, scattered(): return lax.psum_scatter(partial_sum, 'ctx', scatter_dimension=0, tiled=True)  172 us
    reduce_scatter x1, waiting for transfers between devices, local(): lax.psum_scatter(partial_out, 'tp', scatter_dimension=0, tiled=True)  78.2 us
    all_gather x1, waiting for transfers between devices, local(): gathered = lax.all_gather(blocked, 'tp', axis=0, tiled=True)  75 us
    all_to_all x1, blocking collectives, local(): lax.all_to_all(gathered, 'ctx', split_axis=0, concat_axis=0, tiled=True)  52.8 us
    dot_general x3, matrix products, stream(): jnp.dot(operand, w_feature[:, p], preferred_element_type=jnp.float32)  41.6 us
    pallas_call x1, Pallas kernels, out_projection(): pl.pallas_call(out_kernel, grid=(slabs * per,), in_specs=[whole(q), whole...  23.7 us
    pallas_call x1, Pallas kernels, long_filtering(): pl.pallas_call(long_kernel, grid=(width // LANES,), in_specs=[spec, pl.Bl...  11.7 us
  transfers between devices with their start and end apart: 9, of which 6 were waited for; matrix products, arithmetic and copies ran while one was open for 6% of the time, Pallas kernels for 5%

profile of v1, /device:TPU:0, one launch (start us, length us, event | category | flops | bytes accessed | tf_op | source)
XLA Modules:
  0.0 501.7 jit_solution(11869183351841215125)
XLA Ops:
  6.5 0.0 copy-start.5
  6.5 0.0 all-gather.2.cloned.1.call-start
  6.5 1.5 copy.8
  8.0 1.3 copy.9
  9.3 0.0 all-gather.2.cloned.1.call-update
  9.4 0.0 reduce-scatter.7.cloned.1.call-start
  9.4 0.0 copy-done.5
  9.4 0.1 rev.3
  9.5 0.1 pad_convert_fusion.row_ref
  9.6 8.4 %toeplitz.1.t_ref = bf16[128,128,256]{2,1,0:T(8,128)(2,1)} custom-call(f32[128,256]{1,0:T(8,128)S(1)} %pad_convert_fusion.row_ref), custom_call_target="tpu_custom_call" | custom-call | tf_op jit(solution)/shard_map/toeplitz/pallas_call | solution.py:38
  18.0 75.0 %all-gather.2.cloned.1.call-done = bf16[8,256,1024]{2,1,0:T(8,128)(2,1)} async-done(((bf16[2,256,1024]{2,1,0:T(8,128)(2,1)}), bf16[8,256,1024]{2,1,0:T(8,128)(2,1)}) %all-gather.2.cloned.1.call-update) | async-done | bytes 4194320 | tf_op jit(solution)/shard_map/all_gather | solution.py:166
  93.0 52.8 %all_to_all.5 = bf16[8,256,1024]{2,1,0:T(8,128)(2,1)S(1)} all-to-all(bf16[8,256,1024]{2,1,0:T(8,128)(2,1)} %all-gather.2.cloned.1.call-done), channel_id=1, replica_groups=mesh['ctx'=8,'tp'=4] {'ctx'}, dimensions={0} | all-to-all | bytes 8388608 | tf_op jit(solution)/shard_map/all_to_all | solution.py:169
  145.7 0.0 copy-start.3
  145.8 2.1 copy-done.3
  147.8 13.0 %convolution_convert_fusion.1 = bf16[2048,2048]{1,0:T(8,128)(2,1)} fusion(bf16[2048,1024]{1,0:T(8,128)(2,1)S(1)} %bitcast.23, bf16[1024,3,2048]{2,0,1:T(8,128)(2,1)} %param.6), kind=kOutput, calls=%fused_computation.1 | convolution fusion | flops 8594128896 | bytes 16777216 | tf_op jit(solution)/shard_map/dot_general | solution.py:173
  160.8 0.0 reduce-scatter.7.cloned.1.call-update
  160.9 0.0 reduce-scatter.9.cloned.1.call-start
  160.9 14.6 %convolution_convert_fusion = bf16[2048,2048]{1,0:T(8,128)(2,1)} fusion(bf16[2048,1024]{1,0:T(8,128)(2,1)} %bitcast.24, bf16[1024,3,2048]{2,0,1:T(8,128)(2,1)} %param.6), kind=kOutput, calls=%fused_computation | convolution fusion | flops 8594128896 | bytes 16777216 | tf_op jit(solution)/shard_map/dot_general | solution.py:173
  175.5 0.0 reduce-scatter.9.cloned.1.call-update
  175.6 0.0 reduce-scatter.5.cloned.1.call-start
  175.6 13.9 %convolution_convert_fusion.2 = bf16[2048,2048]{1,0:T(8,128)(2,1)} fusion(bf16[2048,1024]{1,0:T(8,128)(2,1)} %bitcast.25, bf16[1024,3,2048]{2,0,1:T(8,128)(2,1)} %param.6), kind=kOutput, calls=%fused_computation.2 | convolution fusion | flops 8594128896 | bytes 16777216 | tf_op jit(solution)/shard_map/dot_general | solution.py:173
  189.6 0.0 copy-start.4
  189.6 0.0 reduce-scatter.5.cloned.1.call-update
  189.6 0.0 reduce-scatter.11.cloned.1.call-start
  189.6 39.3 %reduce-scatter.7.cloned.1.call-done.k_ref = bf16[256,2048]{1,0:T(8,128)(2,1)} async-done(((bf16[2048,2048]{1,0:T(8,128)(2,1)}), bf16[256,2048]{1,0:T(8,128)(2,1)}) %reduce-scatter.7.cloned.1.call-update) | async-done | bytes 1048592 | tf_op jit(solution)/shard_map/reduce_scatter | solution.py:179
  229.0 0.8 slice.41
  229.8 1.7 collective-permute-start.1
  231.5 72.6 %reduce-scatter.9.cloned.1.call-done.v_ref = bf16[256,2048]{1,0:T(8,128)(2,1)} async-done(((bf16[2048,2048]{1,0:T(8,128)(2,1)}), bf16[256,2048]{1,0:T(8,128)(2,1)}) %reduce-scatter.9.cloned.1.call-update) | async-done | bytes 1048592 | tf_op jit(solution)/shard_map/reduce_scatter | solution.py:179
  304.2 0.8 slice.42
  305.0 1.9 collective-permute-start.2
  306.9 0.0 copy-done.4
  306.9 0.0 collective-permute-done.1.kr_ref
  307.0 0.7 collective-permute-done.2.vr_ref
  307.6 0.0 copy-start.1
  307.6 1.2 copy-done.1
  308.8 0.0 copy-start.2
  308.8 1.2 copy-done.2
  310.1 5.0 gate.1.g_ref
  315.1 4.0 collective-permute-start.3
  319.1 59.7 %reduce-scatter.5.cloned.1.call-done.q_ref = bf16[256,2048]{1,0:T(8,128)(2,1)} async-done(((bf16[2048,2048]{1,0:T(8,128)(2,1)}), bf16[256,2048]{1,0:T(8,128)(2,1)}) %reduce-scatter.5.cloned.1.call-update) | async-done | bytes 1048592 | tf_op jit(solution)/shard_map/reduce_scatter | solution.py:179
  378.8 0.8 slice.40
  379.7 0.0 copy-start
  379.7 1.9 collective-permute-start
  381.5 0.0 collective-permute-done.3.r_ref
  381.5 11.7 %long.1.l_ref = f32[256,2048]{1,0:T(8,128)S(1)} custom-call(bf16[256,2048]{1,0:T(8,128)(2,1)S(1)} %gate.1.g_ref, bf16[128,2048]{1,0:T(8,128)(2,1)S(1)} %collective-permute-done.3.r_ref, bf16[128,128,256]{2,1,0:T(8,128)(2,1)} %toeplitz.1.t_ref), custom_call_target="tpu_custom_call" | custom-call | flops 2147483648 | bytes 12582912 | tf_op jit(solution)/shard_map/long/pallas_call | solution.py:103
  393.2 0.0 collective-permute-done.qr_ref
  393.3 0.0 copy-done
  393.3 23.7 %out.1 = bf16[4,256,2048]{2,1,0:T(8,128)(2,1)} custom-call(bf16[256,2048]{1,0:T(8,128)(2,1)S(1)} %copy-done, bf16[16,2048]{1,0:T(8,128)(2,1)S(1)} %collective-permute-done.qr_ref, f32[7,2048]{1,0:T(8,128)S(1)} %get-tuple-element.10.qt_ref, f32[256,2048]{1,0:T(8,128)S(1)} %long.1.l_ref, bf16[2048,8192]{1,0:T(8,128)(2,1)} %w_ref.1), custom_call_target="tpu_custom_call" | custom-call | tf_op jit(solution)/shard_map/out/pallas_call | solution.py:144
  416.9 0.0 reduce-scatter.11.cloned.1.call-update
  417.0 78.2 %reduce-scatter.11.cloned.1.call-done = bf16[1,256,2048]{2,1,0:T(8,128)(2,1)} async-done(((bf16[4,256,2048]{2,1,0:T(8,128)(2,1)}), bf16[1,256,2048]{2,1,0:T(8,128)(2,1)}) %reduce-scatter.11.cloned.1.call-update) | async-done | bytes 1048592 | tf_op jit(solution)/shard_map/reduce_scatter | solution.py:191
  (2 shorter events, 0.1 us)
Async XLA Ops:
  6.5 2.9 copy-start.5
  6.5 86.5 %all-gather.2.cloned.1.call-start = ((), (), s32[]{:S(2)}) async-start(), calls=%async_computation.5 | async-start | bytes 5242880 | tf_op jit(solution)/shard_map/all_gather | solution.py:166
  9.4 219.6 %reduce-scatter.7.cloned.1.call-start = ((), (), s32[]{:S(2)}) async-start(), calls=%async_computation.7 | async-start | bytes 9437184 | tf_op jit(solution)/shard_map/reduce_scatter | solution.py:179
  145.7 2.1 copy-start.3
  160.9 143.3 %reduce-scatter.9.cloned.1.call-start = ((), (), s32[]{:S(2)}) async-start(), calls=%async_computation.8 | async-start | bytes 9437184 | tf_op jit(solution)/shard_map/reduce_scatter | solution.py:179
  175.6 203.2 %reduce-scatter.5.cloned.1.call-start = ((), (), s32[]{:S(2)}) async-start(), calls=%async_computation.6 | async-start | bytes 9437184 | tf_op jit(solution)/shard_map/reduce_scatter | solution.py:179
  189.6 117.4 %copy-start.4 = (f32[7,3,2048]{2,0,1:T(8,128)S(1)}, f32[7,3,2048]{2,0,1:T(8,128)}, u32[]{:S(2)}) copy-start(f32[7,3,2048]{2,0,1:T(8,128)} %param.7) | copy-start | bytes 516100
  189.6 305.6 %reduce-scatter.11.cloned.1.call-start = ((), (), s32[]{:S(2)}) async-start(), calls=%async_computation.9 | async-start | bytes 5242880 | tf_op jit(solution)/shard_map/reduce_scatter | solution.py:191
  229.8 77.1 %collective-permute-start.1 = (bf16[16,2048]{1,0:T(8,128)(2,1)S(1)}, bf16[16,2048]{1,0:T(8,128)(2,1)S(1)}, u32[]{:S(2)}, u32[]{:S(2)}) collective-permute-start(bf16[16,2048]{1,0:T(8,128)(2,1)S(1)} %slice.41), channel_id=1, source_target_pairs={{0,4},{4,8},{8,12},{12,16},{16,20},{20,24},{24,28},{1,5},{5,9},{9,... | collective-permute-start | bytes 196616 | tf_op jit(solution)/shard_map/ppermute | solution.py:25
  305.0 2.6 collective-permute-start.2
  307.6 1.2 copy-start.1
  308.8 1.2 copy-start.2
  315.1 66.4 %collective-permute-start.3 = (bf16[128,2048]{1,0:T(8,128)(2,1)S(1)}, bf16[128,2048]{1,0:T(8,128)(2,1)S(1)}, u32[]{:S(2)}, u32[]{:S(2)}) collective-permute-start(bf16[128,2048]{1,0:T(8,128)(2,1)S(1)} %slice.43), channel_id=1, source_target_pairs={{0,4},{4,8},{8,12},{12,16},{16,20},{20,24},{24,28},{1,5},{5,9},{9,... | collective-permute-start | bytes 1572872 | tf_op jit(solution)/shard_map/ppermute | solution.py:25
  379.7 13.6 %copy-start = (bf16[256,2048]{1,0:T(8,128)(2,1)S(1)}, bf16[256,2048]{1,0:T(8,128)(2,1)}, u32[]{:S(2)}) copy-start(bf16[256,2048]{1,0:T(8,128)(2,1)} %reduce-scatter.5.cloned.1.call-done.q_ref) | copy-start | bytes 3145732
  379.7 13.6 %collective-permute-start = (bf16[16,2048]{1,0:T(8,128)(2,1)S(1)}, bf16[16,2048]{1,0:T(8,128)(2,1)S(1)}, u32[]{:S(2)}, u32[]{:S(2)}) collective-permute-start(bf16[16,2048]{1,0:T(8,128)(2,1)S(1)} %slice.40), channel_id=1, source_target_pairs={{0,4},{4,8},{8,12},{12,16},{16,20},{20,24},{24,28},{1,5},{5,9},{9,... | collective-permute-start | bytes 196616 | tf_op jit(solution)/shard_map/ppermute | solution.py:25
Sparse Core Ops, SparseCore 0:
  9.5 83.4 all-gather.1
  161.0 67.9 reduce-scatter.6
  232.8 71.2 reduce-scatter.8
  307.5 71.2 reduce-scatter.4
  417.1 78.0 reduce-scatter.10

commit v2 on v1

--- a/solution.py
+++ b/solution.py
@@ -156,6 +156,145 @@
     )(q, q_rim, q_taps, long_out, w_out)
 
 
+def flipped(index, bit):
+    value = 1 << bit
+    return index + value - 2 * value * (index // value % 2)
+
+
+def feature_kernel(n, bits, tiles, x_ref, w_ref, out_ref, *scratch):
+    own, held, sent, got = (
+        scratch[0], scratch[1:bits], scratch[bits : 2 * bits], scratch[2 * bits : 3 * bits]
+    )
+    send_sem, recv_sem = scratch[3 * bits :]
+    step = pl.program_id(0)
+    me = lax.axis_index("ctx")
+    rows = x_ref.shape[0] // n
+    half = w_ref.shape[2] // 2
+    orders = (list(range(1, bits)), list(range(2, bits)) + [1])
+
+    def copy_of(stage, sub, chunk):
+        bit = 0 if stage == 0 else orders[sub][stage - 1]
+        slot = chunk % 2
+        return pltpu.make_async_remote_copy(
+            src_ref=sent[stage].at[slot, sub],
+            dst_ref=got[stage].at[chunk, sub],
+            send_sem=send_sem.at[stage, sub, slot],
+            recv_sem=recv_sem.at[stage, sub, chunk],
+            device_id={"ctx": flipped(me, bit)},
+            device_id_type=pl.DeviceIdType.MESH,
+        )
+
+    @pl.when(step == 0)
+    def _():
+        barrier = pltpu.get_barrier_semaphore()
+        for bit in range(bits):
+            pl.semaphore_signal(
+                barrier, inc=1, device_id={"ctx": flipped(me, bit)},
+                device_id_type=pl.DeviceIdType.MESH,
+            )
+        pl.semaphore_wait(barrier, bits)
+
+    @pl.when(step < tiles)
+    def _():
+        slot = step % 2
+        for mine in (0, 1):
+            target_ref = own if mine else sent[0]
+            for m in range(n // 2):
+                r = 2 * m + 1 - mine
+                target = me
+                for bit in range(bits):
+                    if r >> bit & 1:
+                        target = flipped(target, bit)
+                block = x_ref[pl.ds(pl.multiple_of(target * rows, rows), rows), :]
+                product = jnp.dot(
+                    block, w_ref[0], preferred_element_type=jnp.float32
+                ).astype(jnp.bfloat16)
+                for sub in (0, 1):
+                    place = 0
+                    for bit in orders[sub]:
+                        place = 2 * place + (r >> bit & 1)
+                    target_ref[slot, sub, place * rows : (place + 1) * rows] = product[
+                        :, sub * half : (sub + 1) * half
+                    ]
+            if not mine:
+                for sub in (0, 1):
+                    copy_of(0, sub, step).start()
+
+    for stage in range(1, bits + 1):
+        chunk = step - stage
+
+        @pl.when(jnp.logical_and(chunk >= 0, chunk < tiles))
+        def _():
+            slot = chunk % 2
+            before = own if stage == 1 else held[stage - 2]
+            keep = rows * (n >> (stage + 1))
+            for sub in (0, 1):
+                copy_of(stage - 1, sub, chunk).wait()
+                for part in ((1, 0) if stage < bits else (0,)):
+                    size = keep if stage < bits else rows
+                    at = slice(part * size, (part + 1) * size)
+                    total = before[slot, sub, at].astype(jnp.float32) + got[stage - 1][
+                        chunk, sub, at
+                    ].astype(jnp.float32)
+                    if stage == bits:
+                        out_ref[0, :, sub * half : (sub + 1) * half] = total.astype(out_ref.dtype)
+                    elif part:
+                        sent[stage][slot, sub] = total.astype(jnp.bfloat16)
+                        copy_of(stage, sub, chunk).start()
+                    else:
+                        held[stage - 1][slot, sub] = total
+
+
+def featurizer(x, w, n):
+    bits = n.bit_length() - 1
+    assert n == 1 << bits and bits >= 2
+    rows = x.shape[0] // n
+    streams, depth, width = w.shape
+    tile = min(width, 512)
+    half = tile // 2
+    per = width // tile
+    tiles = streams * per
+
+    def into(i):
+        i = jnp.minimum(i, tiles - 1)
+        return i // per, 0, i % per
+
+    def outof(i):
+        i = jnp.maximum(i - bits, 0)
+        return i // per, 0, i % per
+
+    def buffer(slots, blocks, dtype):
+        return pltpu.VMEM((slots, 2, blocks * rows, half), dtype)
+
+    return pl.pallas_call(
+        functools.partial(feature_kernel, n, bits, tiles),
+        grid=(tiles + bits,),
+        in_specs=[
+            pl.BlockSpec(x.shape, lambda i: (0, 0)),
+            pl.BlockSpec((1, depth, tile), into),
+        ],
+        out_specs=pl.BlockSpec((1, rows, tile), outof),
+        out_shape=jax.ShapeDtypeStruct((streams, rows, width), jnp.bfloat16),
+        scratch_shapes=[buffer(2, n // 2, jnp.bfloat16)]
+        + [buffer(2, n >> (s + 1), jnp.float32) for s in range(1, bits)]
+        + [buffer(2, n >> (s + 1), jnp.bfloat16) for s in range(bits)]
+        + [buffer(tiles, n >> (s + 1), jnp.bfloat16) for s in range(bits)]
+        + [
+            pltpu.SemaphoreType.DMA((bits, 2, 2)),
+            pltpu.SemaphoreType.DMA((bits, 2, tiles)),
+        ],
+        compiler_params=pltpu.CompilerParams(
+            vmem_limit_bytes=56 * 1024 * 1024, collective_id=0, has_side_effects=True
+        ),
+        cost_estimate=pl.CostEstimate(
+            flops=2 * x.shape[0] * depth * width * streams,
+            bytes_accessed=2 * w.size,
+            transcendentals=0,
+        ),
+        name="featurizer",
+    )(x, w)
+
+
 def local(hidden, w_feature, short_filter, mr_filter, w_out):
     rows = hidden.shape[0]
     feature_block = w_feature.shape[0]
@@ -169,24 +308,13 @@
     columns = lax.all_to_all(gathered, "ctx", split_axis=0, concat_axis=0, tiled=True)
     columns = columns.reshape(n_ctx * rows, feature_block)
 
-    def stream(p, operand):
-        partial_sum = jnp.dot(
-            operand, w_feature[:, p], preferred_element_type=jnp.float32
-        ).astype(jnp.bfloat16)
-        return partial_sum
-
-    def scattered(partial_sum):
-        return lax.psum_scatter(partial_sum, "ctx", scatter_dimension=0, tiled=True)
-
-    k = scattered(stream(1, columns))
-    v = scattered(stream(2, columns))
-    q = scattered(stream(0, columns))
-    k_rim = passed_along(k[rows - RIM :], "ctx", 1)
-    v_rim = passed_along(v[rows - RIM :], "ctx", 1)
+    q, k, v = featurizer(columns, jnp.swapaxes(w_feature, 0, 1), n_ctx)
+    q_rim, k_rim, v_rim = passed_along(
+        jnp.stack([q[rows - RIM :], k[rows - RIM :], v[rows - RIM :]]), "ctx", 1
+    )
     gated = gating(k, v, k_rim, v_rim, short_filter[:, 1], short_filter[:, 2])
     gated_rim = passed_along(gated[rows - TAPS_MR :], "ctx", 1)
     long_out = long_filtering(gated, gated_rim, toeplitz)
-    q_rim = passed_along(q[rows - RIM :], "ctx", 1)
     partial_out = out_projection(q, q_rim, short_filter[:, 0], long_out, w_out, n_tp)
     summed = lax.psum_scatter(partial_out, "tp", scatter_dimension=0, tiled=True)
     return summed.reshape(rows, -1)

time: 503 us -> 402 us (0.80)
  waiting for transfers between devices: 326 us -> 210 us
  Pallas kernels: 48.7 us -> 161 us
  blocking collectives: 52.8 us -> 0 us
  matrix products: 41.6 us -> 0 us
    reduce_scatter x3 -> x0, waiting for transfers between devices: 172 us -> none  [scattered(): return lax.psum_scatter(partial_sum, 'ctx', scatter_dimension=0, tiled=True)]
    pallas_call x0 -> x1, Pallas kernels: none -> 112 us  [featurizer(): pl.pallas_call(functools.partial(feature_kernel, n, bits, tiles), grid=(t...]
    all_to_all x1 -> x0, blocking collectives: 52.8 us -> none  [local(): lax.all_to_all(gathered, 'ctx', split_axis=0, concat_axis=0, tiled=True)]
    all_to_all x0 -> x1, waiting for transfers between devices: none -> 49 us  [local(): lax.all_to_all(gathered, 'ctx', split_axis=0, concat_axis=0, tiled=True)]
    dot_general x3 -> x0, matrix products: 41.6 us -> none  [stream(): jnp.dot(operand, w_feature[:, p], preferred_element_type=jnp.float32)]
    reduce_scatter x1, waiting for transfers between devices: 78.2 us -> 84.4 us  [local(): lax.psum_scatter(partial_out, 'tp', scatter_dimension=0, tiled=True)]
  transfers between devices with their start and end apart: 9 -> 5, of which waited for: 6 -> 4; matrix products, arithmetic and copies ran while one was open for 6% -> 1% of each run, Pallas kernels for 5% -> 2%
where the time goes in v2:
time: 402 us; the launch traced here: 401 us
  waiting for transfers between devices  210 us (52%)
  Pallas kernels  161 us (40%)
  between operations  13.5 us (3%)
  starting transfers between devices  10.2 us (3%)
  local copies, waits for them, and re-layouts  6.18 us (2%)
    pallas_call x1, Pallas kernels, featurizer(): pl.pallas_call(functools.partial(feature_kernel, n, bits, tiles), grid=(t...  112 us
    reduce_scatter x1, waiting for transfers between devices, local(): lax.psum_scatter(partial_out, 'tp', scatter_dimension=0, tiled=True)  84.4 us
    all_gather x1, waiting for transfers between devices, local(): gathered = lax.all_gather(blocked, 'tp', axis=0, tiled=True)  75 us
    all_to_all x1, waiting for transfers between devices, local(): lax.all_to_all(gathered, 'ctx', split_axis=0, concat_axis=0, tiled=True)  49 us
    pallas_call x1, Pallas kernels, out_projection(): pl.pallas_call(out_kernel, grid=(slabs * per,), in_specs=[whole(q), whole...  23.7 us
    pallas_call x1, Pallas kernels, long_filtering(): pl.pallas_call(long_kernel, grid=(width // LANES,), in_specs=[spec, pl.Bl...  11.7 us
    pallas_call x1, Pallas kernels, toeplitz_of(): pl.pallas_call(toeplitz_kernel, grid=(groups // per,), in_specs=[pl.Block...  8.45 us
  transfers between devices with their start and end apart: 5, of which 4 were waited for; matrix products, arithmetic and copies ran while one was open for 1% of the time, Pallas kernels for 2%

profile of v2, /device:TPU:0, one launch (start us, length us, event | category | flops | bytes accessed | tf_op | source)
XLA Modules:
  0.0 401.2 jit_solution(11728023801877294885)
XLA Ops:
  6.5 0.0 copy-start.1
  6.5 0.0 all-gather.2.cloned.1.call-start
  6.5 1.5 copy.7
  8.0 1.3 copy.8
  9.3 0.0 all-gather.2.cloned.1.call-update
  9.4 0.0 copy-done.1
  9.4 0.1 rev.3
  9.5 0.1 pad_convert_fusion.row_ref
  9.6 8.4 %toeplitz.1.t_ref = bf16[128,128,256]{2,1,0:T(8,128)(2,1)} custom-call(f32[128,256]{1,0:T(8,128)S(1)} %pad_convert_fusion.row_ref), custom_call_target="tpu_custom_call" | custom-call | tf_op jit(solution)/shard_map/toeplitz/pallas_call | solution.py:38
  18.0 0.0 copy-start
  18.0 75.0 %all-gather.2.cloned.1.call-done = bf16[8,256,1024]{2,1,0:T(8,128)(2,1)} async-done(((bf16[2,256,1024]{2,1,0:T(8,128)(2,1)}), bf16[8,256,1024]{2,1,0:T(8,128)(2,1)}) %all-gather.2.cloned.1.call-update) | async-done | bytes 4194320 | tf_op jit(solution)/shard_map/all_gather | solution.py:305
  93.0 4.6 %all-to-all-start = ((bf16[8,256,1024]{2,1,0:T(8,128)(2,1)}), bf16[8,256,1024]{2,1,0:T(8,128)(2,1)}, u32[]{:S(2)}, u32[]{:S(2)}) async-start(bf16[8,256,1024]{2,1,0:T(8,128)(2,1)} %all-gather.2.cloned.1.call-done), calls=%async_computation | async-start | bytes 8388608 | tf_op jit(solution)/shard_map/all_to_all | solution.py:308
  97.6 0.0 reduce-scatter.2.cloned.1.call-start
  97.6 0.0 copy-done
  97.7 49.0 %all-to-all-done = bf16[8,256,1024]{2,1,0:T(8,128)(2,1)} async-done(((bf16[8,256,1024]{2,1,0:T(8,128)(2,1)}), bf16[8,256,1024]{2,1,0:T(8,128)(2,1)}, u32[]{:S(2)}, u32[]{:S(2)}) %all-to-all-start) | async-done | bytes 4194336 | tf_op jit(solution)/shard_map/all_to_all | solution.py:308
  146.7 112.4 %featurizer.1 = bf16[3,256,2048]{2,1,0:T(8,128)(2,1)} custom-call(bf16[2048,1024]{1,0:T(8,128)(2,1)} %bitcast.2.x_ref, bf16[3,1024,2048]{2,1,0:T(8,128)(2,1)} %bitcast.25), custom_call_target="tpu_custom_call" | custom-call | flops 25769803776 | bytes 12582912 | tf_op jit(solution)/shard_map/featurizer/pallas_call | solution.py:269
  259.1 0.9 slice.24
  260.0 1.3 collective-permute-start
  261.3 2.3 slice_bitcast_fusion
  263.6 0.0 collective-permute-done
  263.6 5.0 %gate.1.g_ref = bf16[256,2048]{1,0:T(8,128)(2,1)S(1)} custom-call(bf16[256,2048]{1,0:T(8,128)(2,1)S(1)} %get-tuple-element.10.k_ref, bf16[256,2048]{1,0:T(8,128)(2,1)S(1)} %get-tuple-element.9.v_ref, bf16[16,2048]{1,0:T(8,128)(2,1)S(1)} %get-tuple-element.16.kr_ref, bf16[16,2048]{1,0:T(8,128)(2,1)S(1)} %get-tuple-element.15.vr_ref, ...), custom_call_target="tpu_custom_call" | custom-call | tf_op jit(solution)/shard_map/gate/pallas_call | solution.py:71
  268.7 4.3 %collective-permute-start.1 = (bf16[128,2048]{1,0:T(8,128)(2,1)S(1)}, bf16[128,2048]{1,0:T(8,128)(2,1)S(1)}, u32[]{:S(2)}, u32[]{:S(2)}) collective-permute-start(bf16[128,2048]{1,0:T(8,128)(2,1)S(1)} %slice.29), channel_id=1, source_target_pairs={{0,4},{4,8},{8,12},{12,16},{16,20},{20,24},{24,28},{1,5},{5,9},{9,... | collective-permute-start | bytes 1572872 | tf_op jit(solution)/shard_map/ppermute | solution.py:25
  273.0 1.5 collective-permute-done.1.r_ref
  274.5 11.7 %long.1.l_ref = f32[256,2048]{1,0:T(8,128)S(1)} custom-call(bf16[256,2048]{1,0:T(8,128)(2,1)S(1)} %gate.1.g_ref, bf16[128,2048]{1,0:T(8,128)(2,1)S(1)} %collective-permute-done.1.r_ref, bf16[128,128,256]{2,1,0:T(8,128)(2,1)} %toeplitz.1.t_ref), custom_call_target="tpu_custom_call" | custom-call | flops 2147483648 | bytes 12582912 | tf_op jit(solution)/shard_map/long/pallas_call | solution.py:103
  286.2 23.7 %out.1 = bf16[4,256,2048]{2,1,0:T(8,128)(2,1)} custom-call(bf16[256,2048]{1,0:T(8,128)(2,1)S(1)} %get-tuple-element.11.q_ref, bf16[16,2048]{1,0:T(8,128)(2,1)S(1)} %get-tuple-element.17.qr_ref, f32[7,2048]{1,0:T(8,128)S(1)} %get-tuple-element.13.qt_ref, f32[256,2048]{1,0:T(8,128)S(1)} %long.1.l_ref, bf16[2048,8192]{1,0:T(8,128)(2,1)} %w_ref.1), custom_call_target="tpu_custom_call" | custom-call | tf_op jit(solution)/shard_map/out/pallas_call | solution.py:144
  309.9 0.0 reduce-scatter.2.cloned.1.call-update
  309.9 84.4 %reduce-scatter.2.cloned.1.call-done = bf16[1,256,2048]{2,1,0:T(8,128)(2,1)} async-done(((bf16[4,256,2048]{2,1,0:T(8,128)(2,1)}), bf16[1,256,2048]{2,1,0:T(8,128)(2,1)}) %reduce-scatter.2.cloned.1.call-update) | async-done | bytes 1048592 | tf_op jit(solution)/shard_map/reduce_scatter | solution.py:319
  (3 shorter events, 0.1 us)
Async XLA Ops:
  6.5 2.8 copy-start.1
  6.5 86.4 %all-gather.2.cloned.1.call-start = ((), (), s32[]{:S(2)}) async-start(), calls=%async_computation.2 | async-start | bytes 5242880 | tf_op jit(solution)/shard_map/all_gather | solution.py:305
  18.0 79.6 %copy-start = (f32[7,3,2048]{2,0,1:T(8,128)S(1)}, f32[7,3,2048]{2,0,1:T(8,128)}, u32[]{:S(2)}) copy-start(f32[7,3,2048]{2,0,1:T(8,128)} %param.7) | copy-start | bytes 516100
  93.0 53.7 %all-to-all-start = ((bf16[8,256,1024]{2,1,0:T(8,128)(2,1)}), bf16[8,256,1024]{2,1,0:T(8,128)(2,1)}, u32[]{:S(2)}, u32[]{:S(2)}) async-start(bf16[8,256,1024]{2,1,0:T(8,128)(2,1)} %all-gather.2.cloned.1.call-done), calls=%async_computation | async-start | bytes 8388608 | tf_op jit(solution)/shard_map/all_to_all | solution.py:308
  97.6 296.8 %reduce-scatter.2.cloned.1.call-start = ((), (), s32[]{:S(2)}) async-start(), calls=%async_computation.3 | async-start | bytes 5242880 | tf_op jit(solution)/shard_map/reduce_scatter | solution.py:319
  260.0 3.6 collective-permute-start
  268.7 5.8 %collective-permute-start.1 = (bf16[128,2048]{1,0:T(8,128)(2,1)S(1)}, bf16[128,2048]{1,0:T(8,128)(2,1)S(1)}, u32[]{:S(2)}, u32[]{:S(2)}) collective-permute-start(bf16[128,2048]{1,0:T(8,128)(2,1)S(1)} %slice.29), channel_id=1, source_target_pairs={{0,4},{4,8},{8,12},{12,16},{16,20},{20,24},{24,28},{1,5},{5,9},{9,... | collective-permute-start | bytes 1572872 | tf_op jit(solution)/shard_map/ppermute | solution.py:25
Sparse Core Ops, SparseCore 0:
  9.5 83.4 all-gather.1
  310.0 84.2 reduce-scatter.1

commit v3 on v2

--- a/solution.py
+++ b/solution.py
@@ -138,7 +138,7 @@
 def out_projection(q, q_rim, q_taps, long_out, w_out, slabs):
     rows, width = q.shape
     slab = w_out.shape[1] // slabs
-    tile = min(slab, 512)
+    tile = min(slab, 1024)
     per = slab // tile
     whole = lambda a: pl.BlockSpec(a.shape, lambda i: (0, 0))
     return pl.pallas_call(

time: 402 us -> 397 us (0.988)
    pallas_call x1, Pallas kernels: 23.7 us -> 19.3 us  [out_projection(): pl.pallas_call(out_kernel, grid=(slabs * per,), in_specs=[whole(q), whole...]
where the time goes in v3:
time: 397 us
  waiting for transfers between devices  210 us (53%)
  Pallas kernels  157 us (40%)
  between operations  13.5 us (3%)
  starting transfers between devices  10.2 us (3%)
  local copies, waits for them, and re-layouts  6.18 us (2%)
    pallas_call x1, Pallas kernels, featurizer(): pl.pallas_call(functools.partial(feature_kernel, n, bits, tiles), grid=(t...  112 us
    reduce_scatter x1, waiting for transfers between devices, local(): lax.psum_scatter(partial_out, 'tp', scatter_dimension=0, tiled=True)  84.4 us
    all_gather x1, waiting for transfers between devices, local(): gathered = lax.all_gather(blocked, 'tp', axis=0, tiled=True)  75 us
    all_to_all x1, waiting for transfers between devices, local(): lax.all_to_all(gathered, 'ctx', split_axis=0, concat_axis=0, tiled=True)  49 us
    pallas_call x1, Pallas kernels, out_projection(): pl.pallas_call(out_kernel, grid=(slabs * per,), in_specs=[whole(q), whole...  19.3 us
    pallas_call x1, Pallas kernels, long_filtering(): pl.pallas_call(long_kernel, grid=(width // LANES,), in_specs=[spec, pl.Bl...  11.7 us
    pallas_call x1, Pallas kernels, toeplitz_of(): pl.pallas_call(toeplitz_kernel, grid=(groups // per,), in_specs=[pl.Block...  8.45 us
  transfers between devices with their start and end apart: 5, of which 4 were waited for; matrix products, arithmetic and copies ran while one was open for 1% of the time, Pallas kernels for 2%

profile of v3, /device:TPU:0, one launch (start us, length us, event | category | flops | bytes accessed | tf_op | source)
XLA Modules:
  0.0 396.8 jit_solution(7938312490034903636)
XLA Ops:
  6.5 0.0 copy-start.1
  6.5 0.0 all-gather.2.cloned.1.call-start
  6.5 1.5 copy.7
  8.0 1.3 copy.8
  9.3 0.0 all-gather.2.cloned.1.call-update
  9.4 0.0 copy-done.1
  9.4 0.1 rev.3
  9.5 0.1 pad_convert_fusion.row_ref
  9.6 8.4 %toeplitz.1.t_ref = bf16[128,128,256]{2,1,0:T(8,128)(2,1)} custom-call(f32[128,256]{1,0:T(8,128)S(1)} %pad_convert_fusion.row_ref), custom_call_target="tpu_custom_call" | custom-call | tf_op jit(solution)/shard_map/toeplitz/pallas_call | solution.py:38
  18.0 0.0 copy-start
  18.0 75.0 %all-gather.2.cloned.1.call-done = bf16[8,256,1024]{2,1,0:T(8,128)(2,1)} async-done(((bf16[2,256,1024]{2,1,0:T(8,128)(2,1)}), bf16[8,256,1024]{2,1,0:T(8,128)(2,1)}) %all-gather.2.cloned.1.call-update) | async-done | bytes 4194320 | tf_op jit(solution)/shard_map/all_gather | solution.py:305
  93.0 4.6 %all-to-all-start = ((bf16[8,256,1024]{2,1,0:T(8,128)(2,1)}), bf16[8,256,1024]{2,1,0:T(8,128)(2,1)}, u32[]{:S(2)}, u32[]{:S(2)}) async-start(bf16[8,256,1024]{2,1,0:T(8,128)(2,1)} %all-gather.2.cloned.1.call-done), calls=%async_computation | async-start | bytes 8388608 | tf_op jit(solution)/shard_map/all_to_all | solution.py:308
  97.6 0.0 reduce-scatter.2.cloned.1.call-start
  97.6 0.0 copy-done
  97.7 49.0 %all-to-all-done = bf16[8,256,1024]{2,1,0:T(8,128)(2,1)} async-done(((bf16[8,256,1024]{2,1,0:T(8,128)(2,1)}), bf16[8,256,1024]{2,1,0:T(8,128)(2,1)}, u32[]{:S(2)}, u32[]{:S(2)}) %all-to-all-start) | async-done | bytes 4194336 | tf_op jit(solution)/shard_map/all_to_all | solution.py:308
  146.7 112.4 %featurizer.1 = bf16[3,256,2048]{2,1,0:T(8,128)(2,1)} custom-call(bf16[2048,1024]{1,0:T(8,128)(2,1)} %bitcast.2.x_ref, bf16[3,1024,2048]{2,1,0:T(8,128)(2,1)} %bitcast.25), custom_call_target="tpu_custom_call" | custom-call | flops 25769803776 | bytes 12582912 | tf_op jit(solution)/shard_map/featurizer/pallas_call | solution.py:269
  259.1 0.9 slice.24
  260.0 1.3 collective-permute-start
  261.3 2.3 slice_bitcast_fusion
  263.6 0.0 collective-permute-done
  263.6 5.0 %gate.1.g_ref = bf16[256,2048]{1,0:T(8,128)(2,1)S(1)} custom-call(bf16[256,2048]{1,0:T(8,128)(2,1)S(1)} %get-tuple-element.10.k_ref, bf16[256,2048]{1,0:T(8,128)(2,1)S(1)} %get-tuple-element.9.v_ref, bf16[16,2048]{1,0:T(8,128)(2,1)S(1)} %get-tuple-element.16.kr_ref, bf16[16,2048]{1,0:T(8,128)(2,1)S(1)} %get-tuple-element.15.vr_ref, ...), custom_call_target="tpu_custom_call" | custom-call | tf_op jit(solution)/shard_map/gate/pallas_call | solution.py:71
  268.7 4.3 %collective-permute-start.1 = (bf16[128,2048]{1,0:T(8,128)(2,1)S(1)}, bf16[128,2048]{1,0:T(8,128)(2,1)S(1)}, u32[]{:S(2)}, u32[]{:S(2)}) collective-permute-start(bf16[128,2048]{1,0:T(8,128)(2,1)S(1)} %slice.29), channel_id=1, source_target_pairs={{0,4},{4,8},{8,12},{12,16},{16,20},{20,24},{24,28},{1,5},{5,9},{9,... | collective-permute-start | bytes 1572872 | tf_op jit(solution)/shard_map/ppermute | solution.py:25
  273.0 1.5 collective-permute-done.1.r_ref
  274.5 11.7 %long.1.l_ref = f32[256,2048]{1,0:T(8,128)S(1)} custom-call(bf16[256,2048]{1,0:T(8,128)(2,1)S(1)} %gate.1.g_ref, bf16[128,2048]{1,0:T(8,128)(2,1)S(1)} %collective-permute-done.1.r_ref, bf16[128,128,256]{2,1,0:T(8,128)(2,1)} %toeplitz.1.t_ref), custom_call_target="tpu_custom_call" | custom-call | flops 2147483648 | bytes 12582912 | tf_op jit(solution)/shard_map/long/pallas_call | solution.py:103
  286.2 19.3 %out.1 = bf16[4,256,2048]{2,1,0:T(8,128)(2,1)} custom-call(bf16[256,2048]{1,0:T(8,128)(2,1)S(1)} %get-tuple-element.11.q_ref, bf16[16,2048]{1,0:T(8,128)(2,1)S(1)} %get-tuple-element.17.qr_ref, f32[7,2048]{1,0:T(8,128)S(1)} %get-tuple-element.13.qt_ref, f32[256,2048]{1,0:T(8,128)S(1)} %long.1.l_ref, bf16[2048,8192]{1,0:T(8,128)(2,1)} %w_ref.1), custom_call_target="tpu_custom_call" | custom-call | tf_op jit(solution)/shard_map/out/pallas_call | solution.py:144
  305.5 0.0 reduce-scatter.2.cloned.1.call-update
  305.5 84.4 %reduce-scatter.2.cloned.1.call-done = bf16[1,256,2048]{2,1,0:T(8,128)(2,1)} async-done(((bf16[4,256,2048]{2,1,0:T(8,128)(2,1)}), bf16[1,256,2048]{2,1,0:T(8,128)(2,1)}) %reduce-scatter.2.cloned.1.call-update) | async-done | bytes 1048592 | tf_op jit(solution)/shard_map/reduce_scatter | solution.py:319
  (3 shorter events, 0.1 us)
Async XLA Ops:
  6.5 2.8 copy-start.1
  6.5 86.4 %all-gather.2.cloned.1.call-start = ((), (), s32[]{:S(2)}) async-start(), calls=%async_computation.2 | async-start | bytes 5242880 | tf_op jit(solution)/shard_map/all_gather | solution.py:305
  18.0 79.6 %copy-start = (f32[7,3,2048]{2,0,1:T(8,128)S(1)}, f32[7,3,2048]{2,0,1:T(8,128)}, u32[]{:S(2)}) copy-start(f32[7,3,2048]{2,0,1:T(8,128)} %param.7) | copy-start | bytes 516100
  93.0 53.7 %all-to-all-start = ((bf16[8,256,1024]{2,1,0:T(8,128)(2,1)}), bf16[8,256,1024]{2,1,0:T(8,128)(2,1)}, u32[]{:S(2)}, u32[]{:S(2)}) async-start(bf16[8,256,1024]{2,1,0:T(8,128)(2,1)} %all-gather.2.cloned.1.call-done), calls=%async_computation | async-start | bytes 8388608 | tf_op jit(solution)/shard_map/all_to_all | solution.py:308
  97.6 292.3 %reduce-scatter.2.cloned.1.call-start = ((), (), s32[]{:S(2)}) async-start(), calls=%async_computation.3 | async-start | bytes 5242880 | tf_op jit(solution)/shard_map/reduce_scatter | solution.py:319
  260.0 3.6 collective-permute-start
  268.7 5.8 %collective-permute-start.1 = (bf16[128,2048]{1,0:T(8,128)(2,1)S(1)}, bf16[128,2048]{1,0:T(8,128)(2,1)S(1)}, u32[]{:S(2)}, u32[]{:S(2)}) collective-permute-start(bf16[128,2048]{1,0:T(8,128)(2,1)S(1)} %slice.29), channel_id=1, source_target_pairs={{0,4},{4,8},{8,12},{12,16},{16,20},{20,24},{24,28},{1,5},{5,9},{9,... | collective-permute-start | bytes 1572872 | tf_op jit(solution)/shard_map/ppermute | solution.py:25
Sparse Core Ops, SparseCore 0:
  9.5 83.4 all-gather.1
  305.6 84.2 reduce-scatter.1
